TPU v7x, 32 devices: a whole 2x2x4 slice. The times are simulated.
32 devices in a mesh: groups: 2 (over y), strip: 4 (over z), visit: 2 (over x), band: 2 (over core).
Axes of the slice: x: 2, y: 2, z: 4, core: 2. Of those that a mesh axis runs over, the one named last changes fastest.
Arguments:
- observed: float32 [256, 128, 512], P(('groups', 'strip', 'visit')), parts along dimension 0, may hold values from -6 to 6
- home_strip: int32 [256, 1], P(('groups', 'strip', 'visit')), parts along dimension 0, may hold values from 0 to 3; in each aligned block of 16 rows (0 to 15, 16 to 31, ...) at most 8 rows name the same one
- column_block: int32 [256], P(('groups', 'strip', 'visit')), parts along dimension 0, may hold values from 0 to 28
- psf_index: int32 [256, 4], P(('groups', 'strip', 'visit')), parts along dimension 0, may hold values from 0 to 7
- psf_coeff: float32 [256, 4, 2], P(('groups', 'strip', 'visit')), parts along dimension 0, may hold values from 0.1 to 0.3
- weight: float32 [256], P(('groups', 'strip', 'visit')), parts along dimension 0, may hold values from 0.5 to 2
- kernels: float32 [8, 2, 17], replicated, may hold values from 0.01764706 to 0.052941177
- sky_model: float32 [1024, 4096], P(('groups', 'strip')), parts along dimension 0, may hold values from 0 to 1.5
Outputs:
- restored: float32 [1024, 4096], P(('groups', 'strip')), parts along dimension 0
There are 2 independent parts, one for each index of `groups`. A program takes and returns all parts, laid end to end along the dimension named above; an argument that names none is the same for every part. Nothing has to cross between parts.
Inputs may be any that keep to these rules, and one draw needn't show every extreme that they name: `home_strip`: among the 16 tiles of one owner device (aligned blocks of 16 tiles), no strip is named more than 8 times; some strip is named exactly 8 times.
All inputs are finite; a program needn't handle non-finite values.
Results may differ from a plain program's by a relative error of at most 0.00014.
Values sent between devices are 32-bit elements; how exact they have to be, the bound alone decides.
A program may use at most 128 MiB of HBM per device.

v0:
```python
import jax
import jax.numpy as jnp
from jax import lax
from jax.sharding import PartitionSpec as P

PW = 4096
SROWS = 128
TW = 512
BLK = 128
R = 8
K = 4
TPD = 16


highest = lax.Precision.HIGHEST
step_size = 0.5


def padded_2(shard, sides, width):
    for axis, dim in sides:
        devices, length = (lax.axis_size(axis), shard.shape[dim])
        up = [(i, (i + 1) % devices) for i in range(devices - 1)]
        down = [(j, i) for i, j in up]
        last = lax.slice_in_dim(shard, length - width, length, axis=dim)
        initial = lax.slice_in_dim(shard, 0, width, axis=dim)
        before = lax.ppermute(last, axis, up)
        after = lax.ppermute(initial, axis, down)
        shard = jnp.concatenate([before, shard, after], axis=dim)
    return shard


def passed_along(value, axis, steps):
    count = lax.axis_size(axis)
    initial, last = (max(0, -steps), min(count, count - steps))
    return lax.ppermute(value, axis, [(source, source + steps) for source in range(initial, last)])


def band_matrix(kernel_taps, height, breadth):
    distance = jnp.arange(breadth)[None, :] - jnp.arange(height)[:, None]
    inside = (distance >= 0) & (distance < kernel_taps.shape[0])
    picked = kernel_taps[jnp.clip(distance, 0, kernel_taps.shape[0] - 1)]
    return jnp.where(inside, picked, jnp.zeros_like(picked))


def build_banks(kernels):
    row_matrices = jax.vmap(lambda k: band_matrix(k, SROWS, SROWS + 2 * R))(kernels[:, 0])
    column_matrices = jax.vmap(lambda k: band_matrix(k, BLK, BLK + 2 * R))(kernels[:, 1])
    return (row_matrices, column_matrices)


def psf_scales(psf_coeff):
    across = (jnp.arange(TW).astype(psf_coeff.dtype) + 0.5) / TW - 0.5
    return psf_coeff[..., 0:1] + psf_coeff[..., 1:2] * across


def forward(windows, row_pick, column_pick, psf_scale):
    row_conv = jnp.einsum("skij,sjc->skic", row_pick, windows, precision=highest)
    block_width = column_pick.shape[-2]
    block_reach = column_pick.shape[-1]
    block_count = psf_scale.shape[-1] // block_width
    blocks = jnp.stack(
        [
            row_conv[..., q * block_width : q * block_width + block_reach]
            for q in range(block_count)
        ],
        axis=2,
    )
    convolved = jnp.einsum("skqic,skbc->skiqb", blocks, column_pick, precision=highest)
    convolved = convolved.reshape(
        row_conv.shape[0], row_conv.shape[1], row_conv.shape[2], psf_scale.shape[-1]
    )
    return jnp.sum(psf_scale[:, :, None, :] * convolved, 1)


def adjoint(weighted, row_pick, column_pick, psf_scale):
    spread = psf_scale[:, :, None, :] * weighted[:, None]
    block_width = column_pick.shape[-2]
    block_reach = column_pick.shape[-1]
    total_cols = spread.shape[-1]
    block_count = total_cols // block_width
    shaped = spread.reshape(
        spread.shape[0], spread.shape[1], spread.shape[2], block_count, block_width
    )
    back_cols = jnp.einsum("skiqb,skbc->skqic", shaped, column_pick, precision=highest)
    extent = total_cols + block_reach - block_width
    summed = jnp.zeros(back_cols.shape[:2] + (back_cols.shape[3], extent), back_cols.dtype)
    for q in range(block_count):
        before = q * block_width
        summed = summed + jnp.pad(
            back_cols[:, :, q], ((0, 0), (0, 0), (0, 0), (before, extent - before - block_reach))
        )
    return jnp.einsum("skij,skic->sjc", row_pick, summed, precision=highest)


def on_device(observed, home_strip, column_block, psf_index, psf_coeff, weight, kernels, sky_model):
    strips = lax.axis_size("strip")
    band_count = lax.axis_size("band")
    capacity = 2 * TPD // strips
    band_id = lax.axis_index("band")
    row_matrices, column_matrices = build_banks(kernels)
    targets = home_strip[:, 0]
    onehot = (targets[:, None] == jnp.arange(strips)[None, :]).astype(jnp.int32)
    arrival = jnp.sum((jnp.cumsum(onehot, 0) - onehot) * onehot, 1)
    per_dest = capacity // band_count
    kept_tile = arrival // per_dest == band_id
    slot_pos = arrival % per_dest
    slots = strips * per_dest
    position = targets * per_dest + slot_pos
    chosen = ((position[:, None] == jnp.arange(slots)[None, :]) & kept_tile[:, None]).astype(
        jnp.int32
    )
    source = jnp.sum(chosen * jnp.arange(TPD)[:, None], 0)
    present = jnp.sum(chosen, 0).astype(jnp.float32)
    sent_tiles = jnp.einsum("ts,tij->sij", chosen.astype(jnp.float32), observed, precision=highest)
    details = jnp.concatenate(
        [
            psf_coeff[source].reshape(slots, 2 * K),
            weight[source][:, None],
            column_block[source][:, None].astype(jnp.float32),
            psf_index[source].astype(jnp.float32),
            present[:, None],
        ],
        1,
    )
    got_tiles, got_details = (
        lax.all_to_all(sent_tiles, "strip", split_axis=0, concat_axis=0, tiled=True),
        lax.all_to_all(details, "strip", split_axis=0, concat_axis=0, tiled=True),
    )
    got_coeff = got_details[:, : 2 * K].reshape(slots, K, 2)
    got_weight = got_details[:, 2 * K] * got_details[:, 3 * K + 2]
    quarters = got_details[:, 2 * K + 1].astype(jnp.int32)
    got_index = got_details[:, 2 * K + 2 : 3 * K + 2].astype(jnp.int32)
    row_pick = row_matrices[got_index]
    column_pick = column_matrices[got_index]
    psf_scale = psf_scales(got_coeff)
    quarter = TW // 4
    block_total = PW // quarter + 1
    full_width = block_total * quarter
    reach = TW + 2 * R
    placing = (
        quarters[:, None, None] + jnp.arange(5)[None, :, None]
        == jnp.arange(block_total)[None, None, :]
    ).astype(jnp.float32)
    rimmed = padded_2(sky_model, (("strip", 0),), R)
    padded = jnp.pad(rimmed, ((0, 0), (R, full_width - PW - R)))
    blocked = padded.reshape(padded.shape[0], block_total, quarter)
    windows = jnp.einsum("tjb,rbc->trjc", placing, blocked, precision=highest)
    windows = windows.reshape(slots, padded.shape[0], 5 * quarter)[:, :, :reach]
    partial_value = forward(windows, row_pick, column_pick, psf_scale)
    weighted = got_weight[:, None, None] * (partial_value - got_tiles)
    tile_grads = adjoint(weighted, row_pick, column_pick, psf_scale)
    widened = jnp.pad(tile_grads, ((0, 0), (0, 0), (0, 5 * quarter - reach)))
    widened = widened.reshape(slots, padded.shape[0], 5, quarter)
    grad_sum = jnp.einsum("tjb,trjc->rbc", placing, widened, precision=highest)
    grad_sum = grad_sum.reshape(padded.shape[0], full_width)
    strip_grad = grad_sum[:, R : R + PW]
    from_above = passed_along(strip_grad[SROWS + R :], "strip", 1)
    from_below = passed_along(strip_grad[:R], "strip", -1)
    middle = strip_grad[R : R + SROWS]
    middle = (
        middle
        + jnp.pad(from_above, ((0, SROWS - R), (0, 0)))
        + jnp.pad(from_below, ((SROWS - R, 0), (0, 0)))
    )
    gradient = lax.psum(middle, ("visit", "band"))
    sky_model = jnp.maximum(sky_model - step_size * gradient, 0.0)
    return sky_model


def solution(mesh):
    placed = (
        P(("groups", "strip", "visit"), None, None),
        P(("groups", "strip", "visit"), None),
        P(("groups", "strip", "visit")),
        P(("groups", "strip", "visit"), None),
        P(("groups", "strip", "visit"), None, None),
        P(("groups", "strip", "visit")),
        P(),
        P(("groups", "strip"), None),
    )
    return jax.shard_map(
        on_device,
        mesh=mesh,
        in_specs=placed,
        out_specs=P(("groups", "strip"), None),
        check_vma=False,
    )
```

profile of v0, /device:TPU:0, one launch (start us, length us, event | category | flops | bytes accessed | tf_op | source)
XLA Modules:
  0.0 473.7 jit_solution(2462954408600404835)
XLA Ops:
  15.0 6.4 %all-to-all-start = ((f32[4,4,15]{2,1,0:T(4,128)}), f32[4,4,15]{2,1,0:T(4,128)S(1)}, u32[]{:S(2)}, u32[]{:S(2)}) async-start(f32[4,4,15]{2,1,0:T(4,128)} %concatenate.13), calls=%async_computation | async-start | bytes 16384 | tf_op jit(solution)/shard_map/all_to_all | solution.py:127
  23.1 3.9 collective-permute-start
  28.5 9.7 %fusion.23 = f32[16,128,512]{2,0,1:T(8,128)} fusion(f32[16,128,512]{2,1,0:T(8,128)} %param.8, s32[16]{0:T(128)S(1)} %fusion.56, pred[16]{0:T(512)(128)(4,1)S(1)} %fusion.55), kind=kOutput, calls=%fused_computation.38 | convolution fusion | flops 201327616 | bytes 8388688 | tf_op jit(solution)/shard_map/ts,tij->sij/dot_general | solution.py:114
  38.4 61.6 %gather_fusion = f32[18432,8]{1,0:T(8,128)} fusion(f32[8,17]{0,1:T(8,128)S(1)} %bitcast.101, s32[18432]{0:T(1024)S(1)} %broadcast_clamp_fusion), kind=kCustom, calls=%fused_computation | custom fusion | bytes 1253376 | tf_op jit(solution)/shard_map/vmap()/gather | solution.py:41
  100.0 6.9 %copy.109 = f32[128,144,8]{1,0,2:T(8,128)S(1)} copy(f32[128,144,8]{2,1,0:T(8,128)} %bitcast.109) | data formatting | bytes 1179648 | tf_op jit(solution)/shard_map/vmap()/gather | solution.py:41
  107.0 61.6 %gather_fusion.6 = f32[18432,8]{1,0:T(8,128)} fusion(f32[8,17]{0,1:T(8,128)S(1)} %bitcast.100, s32[18432]{0:T(1024)S(1)} %broadcast_clamp_fusion), kind=kCustom, calls=%fused_computation.6 | custom fusion | bytes 1253376 | tf_op jit(solution)/shard_map/vmap()/gather | solution.py:41
  168.6 7.6 %copy.149 = f32[128,144,8]{1,0,2:T(8,128)} copy(f32[128,144,8]{2,1,0:T(8,128)} %bitcast.108) | data formatting | bytes 1179648 | tf_op jit(solution)/shard_map/vmap()/gather | solution.py:41
  176.2 6.6 %copy.129 = f32[16,128,512]{2,1,0:T(8,128)} copy(f32[16,128,512]{2,0,1:T(8,128)} %fusion.23) | data formatting | bytes 8388608 | tf_op jit(solution)/shard_map/ts,tij->sij/dot_general | solution.py:114
  182.8 5.7 %all-to-all-start.1 = ((f32[16,128,512]{2,1,0:T(8,128)}), f32[16,128,512]{2,1,0:T(8,128)}, u32[]{:S(2)}, u32[]{:S(2)}) async-start(f32[16,128,512]{2,1,0:T(8,128)} %copy.129), calls=%async_computation.1 | async-start | bytes 8388608 | tf_op jit(solution)/shard_map/all_to_all | solution.py:126
  192.7 4.4 gather_fusion.5
  197.1 4.4 gather_fusion.7
  201.7 2.1 select_maximum_fusion
  203.8 2.5 reshape.284
  206.3 2.5 fusion.27
  208.8 5.9 %copy.124 = f32[16,144,5,128]{3,2,1,0:T(8,128)} copy(f32[16,144,5,128]{3,0,2,1:T(8,128)S(1)} %fusion.27) | data formatting | bytes 11796480 | tf_op jit(solution)/shard_map/tjb,rbc->trjc/transpose | solution.py:147
  214.7 9.1 %reshape.211 = f32[16,144,640]{2,1,0:T(8,128)} reshape(f32[16,144,5,128]{3,2,1,0:T(8,128)} %copy.124) | data formatting | bytes 11796480 | tf_op jit(solution)/shard_map/reshape | solution.py:148
  223.8 19.8 %fusion.20 = f32[16,4,128,528]{2,3,1,0:T(8,128)S(1)} fusion(f32[16,4,128,144]{3,2,1,0:T(8,128)} %bitcast.104, f32[16,144,640]{2,1,0:T(8,128)} %reshape.211), kind=kOutput, calls=%fused_computation.27 | convolution fusion | flops 7474249728 | bytes 27918336 | tf_op jit(solution)/shard_map/skij,sjc->skic/dot_general | solution.py:57
  243.6 6.7 %slice_bitcast_fusion.9 = (f32[16,4,1,128,144]{3,4,1,0,2:T(8,128)}, f32[16,4,1,128,144]{3,4,1,0,2:T(8,128)}, f32[16,4,1,128,144]{3,4,1,0,2:T(8,128)}, f32[16,4,1,128,144]{3,4,1,0,2:T(8,128)}) fusion(f32[16,4,128,528]{2,3,1,0:T(8,128)S(1)} %fusion.20), kind=kLoop, calls=%fused_computation.37 | loop fusion | bytes 37748736 | tf_op jit(solution)/shard_map/stack | solution.py:61
  250.3 24.3 %fusion.10 = f32[16,128,4,128]{1,3,2,0:T(8,128)} fusion(f32[16,4,128,144,1]{3,2,4,1,0:T(8,128)} %bitcast.102, f32[16,4,4,128]{3,2,1,0:T(4,128)S(1)} %multiply_add_fusion, f32[16,4,1,128,144]{3,4,1,0,2:T(8,128)} %get-tuple-element.12, f32[16,4,1,128,144]{3,4,1,0,2:T(8,128)} %get-tuple-element.13, f32[16,4,1,128,144]{3,4,1,0,2:T(8,128)} %get-tuple-element.14, ...), kind=kOutput, calls=%fused_computation.20 | convolution fusion | flops 7269253120 | bytes 27918336 | tf_op jit(solution)/shard_map/skqic,skbc->skiqb/dot_general | solution.py:68
  274.5 5.4 %copy.130 = f32[16,128,512]{2,1,0:T(8,128)} copy(f32[16,128,512]{1,2,0:T(8,128)} %bitcast.112) | data formatting | bytes 8388608 | tf_op jit(solution)/shard_map/reduce_sum | solution.py:72
  280.9 6.7 %subtract_multiply_fusion = f32[16,128,512]{2,1,0:T(8,128)} fusion(f32[16,128,512]{2,1,0:T(8,128)} %copy.130, f32[16,128,512]{2,1,0:T(8,128)} %all-to-all-done.1, f32[16]{0:T(128)S(1)} %fusion.46), kind=kLoop, calls=%fused_computation.40 | loop fusion | flops 2097152 | bytes 12582976 | tf_op jit(solution)/shard_map/mul | solution.py:150
  287.6 5.3 %copy.154 = f32[16,128,512]{1,2,0:T(8,128)} copy(f32[16,128,512]{2,1,0:T(8,128)} %subtract_multiply_fusion) | data formatting | bytes 8388608 | tf_op jit(solution)/shard_map/mul | solution.py:76
  293.0 34.7 %fusion.17 = f32[16,4,4,128,144]{3,4,2,1,0:T(8,128)S(1)} fusion(f32[16,4,128,144,1]{3,2,4,1,0:T(8,128)} %bitcast.103, f32[16,128,4,128]{1,3,2,0:T(8,128)} %bitcast.106, f32[16,4,4,128]{3,2,1,0:T(4,128)S(1)} %multiply_add_fusion), kind=kOutput, calls=%fused_computation.25 | convolution fusion | flops 7251951616 | bytes 27918336 | tf_op jit(solution)/shard_map/skiqb,skbc->skqic/dot_general | solution.py:84
  327.7 7.0 %slice_bitcast_fusion.5 = (f32[16,4,128,144]{2,3,1,0:T(8,128)}, f32[16,4,128,144]{2,3,1,0:T(8,128)}, f32[16,4,128,144]{2,3,1,0:T(8,128)}, f32[16,4,128,144]{2,3,1,0:T(8,128)}) fusion(f32[16,4,4,128,144]{3,4,2,1,0:T(8,128)S(1)} %fusion.17), kind=kLoop, calls=%fused_computation.33 | loop fusion | bytes 37748736 | tf_op jit(solution)/shard_map/squeeze | solution.py:90
  334.7 43.5 %fusion.30 = f32[16,144,528]{2,1,0:T(8,128)S(1)} fusion(f32[16,4,128,144]{3,2,1,0:T(8,128)} %bitcast.105, f32[16,4,128,144]{2,3,1,0:T(8,128)} %get-tuple-element.9, f32[16,4,128,144]{2,3,1,0:T(8,128)} %get-tuple-element.10, f32[16,4,128,144]{2,3,1,0:T(8,128)} %get-tuple-element.8, f32[16,4,128,144]{2,3,1,0:T(8,128)} %get-tuple-element.7), kind=kOutput, calls=%fused_computation.46 | convolution fusion | flops 7487225856 | bytes 28459008 | tf_op jit(solution)/shard_map/skij,skic->sjc/dot_general | solution.py:92
  378.2 3.0 pad.37
  381.2 8.6 %reshape.212 = f32[16,144,5,128]{3,2,1,0:T(8,128)} reshape(f32[16,144,640]{2,1,0:T(8,128)} %pad.37) | data formatting | bytes 11796480 | tf_op jit(solution)/shard_map/reshape | solution.py:153
  389.8 9.3 %fusion.21 = f32[144,128,33,1]{1,2,3,0:T(8,128)S(1)} fusion(f32[16,144,5,128]{3,2,1,0:T(8,128)} %reshape.212, s32[16,5]{0,1:T(8,128)S(1)} %iota_add_fusion), kind=kOutput, calls=%fused_computation.28 | convolution fusion | flops 583928384 | bytes 8331584 | tf_op jit(solution)/shard_map/tjb,trjc->rbc/dot_general | solution.py:154
  399.7 3.0 collective-permute-start.2
  405.2 4.4 collective-permute-done.3
  411.5 51.5 %all-reduce.10.cloned.1.call-done = f32[128,4096]{1,0:T(8,128)} async-done(((f32[128,4096]{1,0:T(8,128)}), f32[128,4096]{1,0:T(8,128)}) %all-reduce.10.cloned.1.call-update) | async-done | bytes 2097168 | tf_op jit(solution)/shard_map/psum | solution.py:165
  463.1 3.3 subtract_maximum_fusion
  (67 shorter events, 22.0 us)
Async XLA Ops:
  6.5 5.4 %copy-start = (s32[16]{0:T(128)S(1)}, s32[16]{0:T(128)}, u32[]{:S(2)}) copy-start(s32[16]{0:T(128)} %param.10) | copy-start | bytes 196
  15.0 23.3 %copy-start.4 = (f32[8,2,17]{2,1,0:T(2,128)S(1)}, f32[8,2,17]{2,1,0:T(2,128)}, u32[]{:S(2)}) copy-start(f32[8,2,17]{2,1,0:T(2,128)} %param.14) | copy-start | bytes 3268
  15.0 167.8 %all-to-all-start = ((f32[4,4,15]{2,1,0:T(4,128)}), f32[4,4,15]{2,1,0:T(4,128)S(1)}, u32[]{:S(2)}, u32[]{:S(2)}) async-start(f32[4,4,15]{2,1,0:T(4,128)} %concatenate.13), calls=%async_computation | async-start | bytes 16384 | tf_op jit(solution)/shard_map/all_to_all | solution.py:127
  23.1 178.5 %collective-permute-start = (f32[8,4096]{1,0:T(8,128)}, f32[8,4096]{1,0:T(8,128)S(1)}, u32[]{:S(2)}, u32[]{:S(2)}) collective-permute-start(f32[8,4096]{1,0:T(8,128)} %get-tuple-element.17), channel_id=1, source_target_pairs={{0,4},{4,8},{8,12},{1,5},{5,9},{9,13},{2,6},{6,10},{10,14},{3,7},{... | collective-permute-start | bytes 393224 | tf_op jit(solution)/shard_map/ppermute | solution.py:26
  27.1 174.6 %collective-permute-start.1 = (f32[8,4096]{1,0:T(8,128)}, f32[8,4096]{1,0:T(8,128)S(1)}, u32[]{:S(2)}, u32[]{:S(2)}) collective-permute-start(f32[8,4096]{1,0:T(8,128)} %get-tuple-element.18), channel_id=1, source_target_pairs={{4,0},{8,4},{12,8},{5,1},{9,5},{13,9},{6,2},{10,6},{14,10},{7,3},{... | collective-permute-start | bytes 393224 | tf_op jit(solution)/shard_map/ppermute | solution.py:27
  182.8 98.1 %all-to-all-start.1 = ((f32[16,128,512]{2,1,0:T(8,128)}), f32[16,128,512]{2,1,0:T(8,128)}, u32[]{:S(2)}, u32[]{:S(2)}) async-start(f32[16,128,512]{2,1,0:T(8,128)} %copy.129), calls=%async_computation.1 | async-start | bytes 8388608 | tf_op jit(solution)/shard_map/all_to_all | solution.py:126
  188.5 274.5 %all-reduce.10.cloned.1.call-start = ((), (), s32[]{:S(2)}) async-start(), calls=%async_computation.2 | async-start | bytes 4194304 | tf_op jit(solution)/shard_map/psum | solution.py:165
  197.1 4.6 copy-start.2
  399.5 63.5 %copy-start.3 = (f32[128,4096]{1,0:T(8,128)S(1)}, f32[128,4096]{1,0:T(8,128)}, u32[]{:S(2)}) copy-start(f32[128,4096]{1,0:T(8,128)} %param.15) | copy-start | bytes 6291460
  399.7 5.5 %collective-permute-start.2 = (f32[8,4096]{1,0:T(8,128)S(1)}, f32[8,4096]{1,0:T(8,128)S(1)}, u32[]{:S(2)}, u32[]{:S(2)}) collective-permute-start(f32[8,4096]{1,0:T(8,128)S(1)} %get-tuple-element.15), channel_id=1, source_target_pairs={{0,4},{4,8},{8,12},{1,5},{5,9},{9,13},{2,6},{6,10},{10,14},{3,7},{... | collective-permute-start | bytes 393224 | tf_op jit(solution)/shard_map/ppermute | solution.py:35
  402.7 6.9 %collective-permute-start.3 = (f32[8,4096]{1,0:T(8,128)S(1)}, f32[8,4096]{1,0:T(8,128)S(1)}, u32[]{:S(2)}, u32[]{:S(2)}) collective-permute-start(f32[8,4096]{1,0:T(8,128)S(1)} %get-tuple-element.16), channel_id=1, source_target_pairs={{4,0},{8,4},{12,8},{5,1},{9,5},{13,9},{6,2},{10,6},{14,10},{7,3},{... | collective-permute-start | bytes 393224 | tf_op jit(solution)/shard_map/ppermute | solution.py:35
  409.6 56.8 %copy-start.1 = (s32[16]{0:T(128)S(1)}, s32[16]{0:T(128)}, u32[]{:S(2)}) copy-start(s32[16]{0:T(128)} %param.10) | copy-start | bytes 196
Sparse Core Ops, SparseCore 0:
  411.7 51.3 all-reduce.9
where the time goes:
time: 483 us; the launch traced here: 474 us
  local copies, waits for them, and re-layouts  215 us (45%)
  matrix products  144 us (30%)
  waiting for transfers between devices  58.2 us (12%)
  starting transfers between devices  22.1 us (5%)
  other arithmetic  20 us (4%)
  between operations  14.1 us (3%)
    gather x4, local copies, waits for them, and re-layouts, band_matrix(): picked = kernel_taps[jnp.clip(distance, 0, kernel_taps.shape[0] - 1)]  138 us
    psum x1, waiting for transfers between devices, on_device(): gradient = lax.psum(middle, ('visit', 'band'))  51.5 us
    dot_general x1, matrix products, adjoint(): return jnp.einsum('skij,skic->sjc', row_pick, summed, precision=highest)  43.5 us
    dot_general x1, matrix products, adjoint(): jnp.einsum('skiqb,skbc->skqic', shaped, column_pick, precision=highest)  34.7 us
    dot_general x1, matrix products, forward(): jnp.einsum('skqic,skbc->skiqb', blocks, column_pick, precision=highest)  24.3 us
    dot_general x1, matrix products, forward(): jnp.einsum('skij,sjc->skic', row_pick, windows, precision=highest)  19.8 us
    dot_general x1, matrix products, on_device(): jnp.einsum('ts,tij->sij', chosen.astype(jnp.float32), observed, precision...  9.75 us
  transfers between devices with their start and end apart: 7, of which 4 were waited for; matrix products, arithmetic and copies ran while one was open for 52% of the time, Pallas kernels for 0%

commit v1 on v0

v1 whole, which is shorter than its diff:
```python
import functools

import jax
import jax.numpy as jnp
from jax import lax
from jax.experimental import pallas as pl
from jax.experimental.pallas import tpu as pltpu
from jax.sharding import PartitionSpec as P

PW = 4096
SROWS = 128
TW = 512
R = 8
K = 4
TPD = 16
LANE = 128
REACH = SROWS + 2 * R
MW = PW + 2 * LANE
VIEW = TW + 2 * LANE
EXT = TW + LANE
QROWS = K * LANE + LANE
f32, bf16 = jnp.float32, jnp.bfloat16
step_size = 0.5


def split(x):
    hi = x.astype(bf16)
    return hi, (x - hi.astype(f32)).astype(bf16)


def split_outside(x):
    hi = lax.reduce_precision(x, 8, 7)
    return hi.astype(bf16), (x - hi).astype(bf16)


def banded(taps, height, breadth, offset_of):
    rows = lax.broadcasted_iota(jnp.int32, (1, height, breadth), 1)
    cols = lax.broadcasted_iota(jnp.int32, (1, height, breadth), 2)
    distance = offset_of(rows, cols)
    total = jnp.zeros((taps.shape[0], height, breadth), f32)
    for d in range(taps.shape[1]):
        total = total + jnp.where(distance == d, taps[:, d][:, None, None], 0.0)
    return total


def banks(kernels):
    row = banded(kernels[:, 0], SROWS, REACH, lambda i, j: j - i)
    rowt = banded(kernels[:, 0], REACH, SROWS, lambda j, i: j - i)
    colt = banded(kernels[:, 1], REACH, LANE, lambda c, b: c - b)
    hi, lo = split_outside(row)
    prow = jnp.concatenate([hi, lo, hi], 2)
    prow = jnp.pad(prow, ((0, 0), (0, 0), (0, 512 - 3 * REACH)))
    thi, tlo = split_outside(rowt)
    return prow, thi, tlo, colt


def mm(a, b):
    return lax.dot_general(a, b, (((1,), (0,)), ((), ())), preferred_element_type=f32)


def mmt(a, b):
    return lax.dot_general(a, b, (((1,), (1,)), ((), ())), preferred_element_type=f32)


def tiles_kernel(
    home, block, index, coeff, weight, sky, obs, prow, thi, tlo, colt,
    acc, wcat, pcat, lhi, llo, qhi, qlo, bhi, blo, pthi, ptlo, views, seen, sems,
):
    acc[...] = jnp.zeros_like(acc)
    wcat[...] = jnp.zeros_like(wcat)
    qhi[...] = jnp.zeros_like(qhi)
    qlo[...] = jnp.zeros_like(qlo)
    band = lax.axis_index("band")
    count = TPD // lax.axis_size("band")
    lane = lax.broadcasted_iota(jnp.int32, (SROWS, LANE), 1)
    tail = lane < 2 * R
    across = (lane.astype(f32) + 0.5) / TW - 0.5

    def fetches(i):
        t, slot = band * count + i, i % 2
        top = pl.multiple_of(home[t, 0] * SROWS, SROWS)
        start = pl.multiple_of(block[t] * LANE, LANE)
        return (
            pltpu.make_async_copy(
                sky.at[pl.ds(top, REACH), pl.ds(start, VIEW)], views.at[slot], sems.at[0, slot]
            ),
            pltpu.make_async_copy(obs.at[t], seen.at[slot], sems.at[1, slot]),
        )

    for copy in fetches(0):
        copy.start()

    def one(i, carry):
        t, slot = band * count + i, i % 2

        @pl.when(i + 1 < count)
        def _():
            for copy in fetches(i + 1):
                copy.start()

        for copy in fetches(i):
            copy.wait()
        top = pl.multiple_of(home[t, 0] * SROWS, SROWS)
        start = pl.multiple_of(block[t] * LANE, LANE)
        window = pltpu.roll(views[slot], VIEW - (LANE - R), 1)[:, :EXT]
        whi, wlo = split(window)
        wcat[0:REACH, :] = whi
        wcat[REACH : 2 * REACH, :] = whi
        wcat[2 * REACH : 3 * REACH, :] = wlo
        for k in range(K):
            n = index[t, k]
            pcat[k * SROWS : (k + 1) * SROWS, :] = prow[n]
            pthi[:, k * SROWS : (k + 1) * SROWS] = thi[n]
            ptlo[:, k * SROWS : (k + 1) * SROWS] = tlo[n]
            taps = colt[n]
            for half in range(2):
                hi, lo = split(taps * coeff[t, 2 * k + half])
                side = slice(half * LANE, (half + 1) * LANE)
                qhi[k * LANE : (k + 1) * LANE, side] = hi[:LANE]
                qlo[k * LANE : (k + 1) * LANE, side] = lo[:LANE]
                at = K * LANE + 2 * R * k
                qhi[at : at + 2 * R, side] = hi[LANE:]
                qlo[at : at + 2 * R, side] = lo[LANE:]
        rowed = mm(pcat[...], wcat[...])
        for q in range(TW // LANE):
            rows = slice(q * LANE, (q + 1) * LANE)
            packed = jnp.zeros((SROWS, LANE), f32)
            for k in range(K):
                part = rowed[k * SROWS : (k + 1) * SROWS]
                hi, lo = split(part[:, q * LANE : (q + 1) * LANE])
                lhi[rows, k * LANE : (k + 1) * LANE] = hi
                llo[rows, k * LANE : (k + 1) * LANE] = lo
                end = jnp.where(tail, part[:, (q + 1) * LANE : (q + 2) * LANE], 0.0)
                packed = packed + (pltpu.roll(end, 2 * R * k, 1) if k else end)
            hi, lo = split(packed)
            lhi[rows, K * LANE :] = hi
            llo[rows, K * LANE :] = lo
        both = mm(lhi[...], qhi[...]) + mm(lhi[...], qlo[...]) + mm(llo[...], qhi[...])
        factor = weight[t]
        spread = []
        for q in range(TW // LANE):
            rows = slice(q * LANE, (q + 1) * LANE)
            at = across + q * LANE / TW
            predicted = both[rows, :LANE] + at * both[rows, LANE:]
            weighted = factor * (predicted - seen[slot, :, q * LANE : (q + 1) * LANE])
            spread.append(jnp.concatenate([weighted, at * weighted], 1))
        shi, slo = split(jnp.concatenate(spread, 0))
        back = mmt(shi, qhi[...]) + mmt(shi, qlo[...]) + mmt(slo, qhi[...])
        for m in range(TW // LANE + 1):
            for k in range(K):
                total = 0.0
                if m < TW // LANE:
                    total = back[m * LANE : (m + 1) * LANE, k * LANE : (k + 1) * LANE]
                if m > 0:
                    end = back[(m - 1) * LANE : m * LANE, K * LANE :]
                    end = pltpu.roll(end, LANE - 2 * R * k, 1) if k else end
                    total = total + jnp.where(tail, end, 0.0)
                hi, lo = split(total)
                bhi[k * SROWS : (k + 1) * SROWS, m * LANE : (m + 1) * LANE] = hi
                blo[k * SROWS : (k + 1) * SROWS, m * LANE : (m + 1) * LANE] = lo
        grad = mm(pthi[...], bhi[...]) + mm(pthi[...], blo[...]) + mm(ptlo[...], bhi[...])
        grad = jnp.concatenate([grad, jnp.zeros((REACH, LANE), f32)], 1)
        grad = pltpu.roll(grad, LANE - R, 1)
        here = (pl.ds(top, REACH), pl.ds(start, VIEW))
        acc[here] = acc[here] + grad
        return carry

    lax.fori_loop(0, count, one, 0)


def tile_gradients(home, block, index, coeff, weight, sky, obs, bank):
    vmem = pl.BlockSpec(memory_space=pltpu.VMEM)
    smem = pl.BlockSpec(memory_space=pltpu.SMEM)
    return pl.pallas_call(
        tiles_kernel,
        out_shape=jax.ShapeDtypeStruct(sky.shape, f32),
        in_specs=[smem] * 5 + [pl.BlockSpec(memory_space=pl.ANY)] * 2 + [vmem] * 4,
        out_specs=vmem,
        scratch_shapes=[
            pltpu.VMEM((512, EXT), bf16),
            pltpu.VMEM((K * SROWS, 512), bf16),
            pltpu.VMEM((TW, QROWS), bf16),
            pltpu.VMEM((TW, QROWS), bf16),
            pltpu.VMEM((QROWS, 2 * LANE), bf16),
            pltpu.VMEM((QROWS, 2 * LANE), bf16),
            pltpu.VMEM((K * SROWS, EXT), bf16),
            pltpu.VMEM((K * SROWS, EXT), bf16),
            pltpu.VMEM((REACH, K * SROWS), bf16),
            pltpu.VMEM((REACH, K * SROWS), bf16),
            pltpu.VMEM((2, REACH, VIEW), f32),
            pltpu.VMEM((2, SROWS, TW), f32),
            pltpu.SemaphoreType.DMA((2, 2)),
        ],
        compiler_params=pltpu.CompilerParams(vmem_limit_bytes=56 * 2**20),
    )(home, block, index, coeff.reshape(TPD, 2 * K), weight, sky, obs, *bank)


def on_device(observed, home_strip, column_block, psf_index, psf_coeff, weight, kernels, sky_model):
    visits, bands = lax.axis_size("visit"), lax.axis_size("band")
    piece = PW // (visits * bands)
    at = (lax.axis_index("visit") * bands + lax.axis_index("band")) * piece
    mine = lax.dynamic_slice_in_dim(sky_model, at, piece, 1)
    whole = lax.all_gather(mine, "strip", axis=0, tiled=True)
    whole = lax.all_gather(whole, "visit", axis=0)
    whole = lax.all_gather(whole, "band", axis=1)
    sky = jnp.zeros((whole.shape[2] + 2 * R, MW), f32)
    for v in range(visits):
        for b in range(bands):
            sky = lax.dynamic_update_slice(sky, whole[v, b], (R, LANE + (v * bands + b) * piece))
    bank = banks(kernels)
    grads = tile_gradients(
        home_strip, column_block, psf_index, psf_coeff, weight, sky, observed, bank
    )
    grads = grads[R:-R, LANE:-LANE].reshape(-1, visits, bands, piece).transpose(2, 1, 0, 3)
    grads = lax.psum_scatter(grads, "band", scatter_dimension=0)
    grads = lax.psum_scatter(grads, "visit", scatter_dimension=0)
    grads = lax.psum_scatter(grads, "strip", scatter_dimension=0, tiled=True)
    new = jnp.maximum(mine - step_size * grads, 0.0)
    new = lax.all_gather(new, ("visit", "band"), axis=1, tiled=True)
    return new


def solution(mesh):
    tiles = ("groups", "strip", "visit")
    placed = (
        P(tiles, None, None),
        P(tiles, None),
        P(tiles),
        P(tiles, None),
        P(tiles, None, None),
        P(tiles),
        P(),
        P(("groups", "strip"), None),
    )
    return jax.shard_map(
        on_device,
        mesh=mesh,
        in_specs=placed,
        out_specs=P(("groups", "strip"), None),
        check_vma=False,
    )
```

time: 483 us -> 373 us (0.77); the launches traced: 474 us -> 372 us
  waiting for transfers between devices: 58.2 us -> 259 us
  local copies, waits for them, and re-layouts: 215 us -> 49.4 us
  matrix products: 144 us -> 0 us
  Pallas kernels: 0 us -> 38.4 us
  starting transfers between devices: 22.1 us -> 0.27 us
  other arithmetic: 20 us -> 11.3 us
    gather x11 -> x0, local copies, waits for them, and re-layouts: 150 us -> none  [the longest x4 138 us: band_matrix(): picked = kernel_taps[jnp.clip(distance, 0, kernel_taps.shape[0] - 1)]]
    dot_general x7 -> x0, matrix products: 144 us -> none  [the longest x1 43.5 us: adjoint(): return jnp.einsum('skij,skic->sjc', row_pick, summed, precision=highest)]
    all_gather x0 -> x4, waiting for transfers between devices: none -> 137 us  [the longest x1 57 us: on_device(): whole = lax.all_gather(whole, 'visit', axis=0)]
    reduce_scatter x0 -> x3, waiting for transfers between devices: none -> 122 us  [the longest x1 57.8 us: on_device(): grads = lax.psum_scatter(grads, 'visit', scatter_dimension=0)]
    psum x1 -> x0, waiting for transfers between devices: 51.5 us -> none  [on_device(): gradient = lax.psum(middle, ('visit', 'band'))]
    pallas_call x0 -> x1, Pallas kernels: none -> 38.4 us  [tile_gradients(): pl.pallas_call(tiles_kernel, out_shape=jax.ShapeDtypeStruct(sky.shape, f3...]
    all_to_all x2 -> x0, starting transfers between devices: 12.2 us -> none  [the longest x1 6.45 us: on_device(): lax.all_to_all(details, 'strip', split_axis=0, concat_axis=0, tiled=True)]
    ppermute x4 -> x0, starting transfers between devices: 9.52 us -> none  [the longest x2 4.31 us: passed_along(): lax.ppermute(value, axis, [(source, source + steps) for source in range(i...]
  transfers between devices with their start and end apart: 7 -> 7, of which waited for: 4 -> 7; matrix products, arithmetic and copies ran while one was open for 52% -> 3% of each run, Pallas kernels for 0% -> 0%
where the time goes in v1:
time: 373 us; the launch traced here: 372 us
  waiting for transfers between devices  259 us (69%)
  local copies, waits for them, and re-layouts  49.4 us (13%)
  Pallas kernels  38.4 us (10%)
  between operations  13.7 us (4%)
  other arithmetic  11.3 us (3%)
    reduce_scatter x1, waiting for transfers between devices, on_device(): grads = lax.psum_scatter(grads, 'visit', scatter_dimension=0)  57.8 us
    all_gather x1, waiting for transfers between devices, on_device(): whole = lax.all_gather(whole, 'visit', axis=0)  57 us
    all_gather x1, waiting for transfers between devices, on_device(): whole = lax.all_gather(mine, 'strip', axis=0, tiled=True)  49.1 us
    reduce_scatter x1, waiting for transfers between devices, on_device(): grads = lax.psum_scatter(grads, 'strip', scatter_dimension=0, tiled=True)  46 us
    pallas_call x1, Pallas kernels, tile_gradients(): pl.pallas_call(tiles_kernel, out_shape=jax.ShapeDtypeStruct(sky.shape, f3...  38.4 us
    reshape x2, local copies, waits for them, and re-layouts, on_device(): grads[R:-R, LANE:-LANE].reshape(-1, visits, bands, piece)  23.2 us
    all_gather x1, waiting for transfers between devices, on_device(): new = lax.all_gather(new, ('visit', 'band'), axis=1, tiled=True)  22.1 us
    reduce_scatter x1, waiting for transfers between devices, on_device(): grads = lax.psum_scatter(grads, 'band', scatter_dimension=0)  18.1 us
  transfers between devices with their start and end apart: 7, of which 7 were waited for; matrix products, arithmetic and copies ran while one was open for 3% of the time, Pallas kernels for 0%

profile of v1, /device:TPU:0, one launch (start us, length us, event | category | flops | bytes accessed | tf_op | source)
XLA Modules:
  0.0 372.2 jit_solution(3569250197459633945)
XLA Ops:
  6.6 1.9 constant_dynamic-slice_fusion
  8.5 0.0 all-gather.11.cloned.1.call-start
  8.6 49.1 %all-gather.7.cloned.1.call-done = f32[512,1024]{1,0:T(8,128)} async-done(((f32[128,1024]{1,0:T(8,128)}), f32[512,1024]{1,0:T(8,128)}) %all-gather.7.cloned.1.call-update) | async-done | bytes 2097168 | tf_op jit(solution)/shard_map/all_gather | solution.py:203
  57.7 57.0 %all-gather.11.cloned.1.call-done = f32[1024,1024]{1,0:T(8,128)} async-done(((f32[512,1024]{1,0:T(8,128)}), f32[1024,1024]{1,0:T(8,128)}) %all-gather.11.cloned.1.call-update) | async-done | bytes 4194320 | tf_op jit(solution)/shard_map/all_gather | solution.py:204
  114.7 0.7 copy.13.home
  115.4 0.7 copy.14.index
  116.1 0.7 copy.15.coeff
  117.1 0.4 slice_reduce_fusion.33
  117.6 0.4 slice_reduce_fusion.16
  118.3 1.7 fusion.6
  120.0 0.1 reduce-precision_convert_fusion
  120.1 1.6 fusion.8.prow
  121.7 2.2 fusion.9
  123.9 0.7 reduce-precision_convert_fusion.1.thi
  124.7 2.4 select_add_fusion.1.colt
  127.1 9.0 %all-gather.13.cloned.1.call-done = f32[2,1024,1024]{2,1,0:T(8,128)} async-done(((f32[2,512,1024]{2,1,0:T(8,128)}), f32[2,1024,1024]{2,1,0:T(8,128)}) %all-gather.13.cloned.1.call-update) | async-done | bytes 8388624 | tf_op jit(solution)/shard_map/all_gather | solution.py:205
  136.1 1.9 slice_bitcast_fusion.3
  138.0 4.3 %dynamic_update_slice.12 = f32[528,4352]{1,0:T(8,128)} pad(f32[512,1024]{1,0:T(8,128)S(1)} %slice_bitcast_fusion.3, f32[]{:T(128)} %constant.31.clone.1), padding=8_8x128_3200 | pad | bytes 11288580 | tf_op jit(solution)/shard_map/dynamic_update_slice | solution.py:209
  142.3 1.5 fusion.5
  143.8 1.5 fusion.4
  145.3 1.5 fusion.3.sky
  146.8 38.4 %shard_map.82 = f32[528,4352]{1,0:T(8,128)} custom-call(s32[16,1]{1,0:T(8,128)} %copy.13.home, s32[16]{0:T(128)} %block.1, s32[16,4]{1,0:T(8,128)} %copy.14.index, f32[16,8]{1,0:T(8,128)} %copy.15.coeff, f32[16]{0:T(128)} %weight.1, f32[528,4352]{1,0:T(8,128)} %fusion.3.sky, f32[16,128,512]{2,1,0:T(8,128)} %obs.1, bf16[8,128,512]{2,1,0:T(8,128)(2,1)} %fusion.8.prow, ...), custom_call_target="tpu_custom_call" | custom-call | tf_op jit(solution)/shard_map/pallas_call | solution.py:174
  185.2 7.6 %slice.186 = f32[512,4096]{1,0:T(8,128)} slice(f32[528,4352]{1,0:T(8,128)} %shard_map.82), slice={[8:520], [128:4224]} | slice | bytes 16777216 | tf_op jit(solution)/shard_map/slice | solution.py:214
  192.9 11.7 %reshape.189 = f32[512,2,2,1024]{3,2,1,0:T(2,128)} reshape(f32[512,4096]{1,0:T(8,128)} %slice.186) | data formatting | bytes 16777216 | tf_op jit(solution)/shard_map/reshape | solution.py:214
  204.6 11.4 %copy.18 = f32[512,2,2,1024]{3,0,1,2:T(8,128)} copy(f32[512,2,2,1024]{3,2,1,0:T(2,128)} %reshape.189) | data formatting | bytes 16777216 | tf_op jit(solution)/shard_map/reshape | solution.py:214
  216.1 0.0 reduce-scatter.6.cloned.1.call-start
  216.1 18.1 %reduce-scatter.4.cloned.1.call-done = f32[1,2,512,1024]{3,2,1,0:T(8,128)} async-done(((f32[2,2,512,1024]{3,2,1,0:T(8,128)}), f32[1,2,512,1024]{3,2,1,0:T(8,128)}) %reduce-scatter.4.cloned.1.call-update) | async-done | bytes 4194320 | tf_op jit(solution)/shard_map/reduce_scatter | solution.py:215
  234.3 57.8 %reduce-scatter.6.cloned.1.call-done = f32[1,512,1024]{2,1,0:T(8,128)} async-done(((f32[2,512,1024]{2,1,0:T(8,128)}), f32[1,512,1024]{2,1,0:T(8,128)}) %reduce-scatter.6.cloned.1.call-update) | async-done | bytes 2097168 | tf_op jit(solution)/shard_map/reduce_scatter | solution.py:216
  292.1 46.0 %reduce-scatter.8.cloned.1.call-done = f32[128,1024]{1,0:T(8,128)} async-done(((f32[512,1024]{1,0:T(8,128)}), f32[128,1024]{1,0:T(8,128)}) %reduce-scatter.8.cloned.1.call-update) | async-done | bytes 524304 | tf_op jit(solution)/shard_map/reduce_scatter | solution.py:217
  338.1 2.1 subtract_maximum_fusion
  340.2 22.1 %all-gather.9.cloned.1.call-done = f32[128,4096]{1,0:T(8,128)} async-done(((f32[128,1024]{1,0:T(8,128)}), f32[128,4096]{1,0:T(8,128)}) %all-gather.9.cloned.1.call-update) | async-done | bytes 2097168 | tf_op jit(solution)/shard_map/all_gather | solution.py:219
  362.3 3.1 copy.23
  (44 shorter events, 0.8 us)
Async XLA Ops:
  6.5 108.2 %copy-start.3 = (s32[16,1]{0,1:T(1,128)S(1)}, s32[16,1]{0,1:T(1,128)}, u32[]{:S(2)}) copy-start(s32[16,1]{0,1:T(1,128)} %param.9) | copy-start | bytes 196
  6.5 108.9 %copy-start.2 = (s32[16,4]{0,1:T(4,128)S(1)}, s32[16,4]{0,1:T(4,128)}, u32[]{:S(2)}) copy-start(s32[16,4]{0,1:T(4,128)} %param.11) | copy-start | bytes 772
  6.5 109.5 %copy-start.1 = (f32[16,4,2]{0,2,1:T(2,128)S(1)}, f32[16,4,2]{0,2,1:T(2,128)}, u32[]{:S(2)}) copy-start(f32[16,4,2]{0,2,1:T(2,128)} %param.12) | copy-start | bytes 1540
  6.5 110.6 %copy-start = (f32[8,2,17]{2,1,0:T(2,128)S(1)}, f32[8,2,17]{2,1,0:T(2,128)}, u32[]{:S(2)}) copy-start(f32[8,2,17]{2,1,0:T(2,128)} %param.14) | copy-start | bytes 3268
  6.5 51.1 %all-gather.7.cloned.1.call-start = ((), (), s32[]{:S(2)}) async-start(), calls=%async_computation.3 | async-start | bytes 2621440 | tf_op jit(solution)/shard_map/all_gather | solution.py:203
  8.5 106.1 %all-gather.11.cloned.1.call-start = ((), (), s32[]{:S(2)}) async-start(), calls=%async_computation.8 | async-start | bytes 6291456 | tf_op jit(solution)/shard_map/all_gather | solution.py:204
  57.6 78.5 %all-gather.13.cloned.1.call-start = ((), (), s32[]{:S(2)}) async-start(), calls=%async_computation.9 | async-start | bytes 12582912 | tf_op jit(solution)/shard_map/all_gather | solution.py:205
  114.7 119.5 %reduce-scatter.4.cloned.1.call-start = ((), (), s32[]{:S(2)}) async-start(), calls=%async_computation.4 | async-start | bytes 12582912 | tf_op jit(solution)/shard_map/reduce_scatter | solution.py:215
  136.1 6.2 %slice-start = ((s8[8388608]{0:T(1024)(128)(4,1)}), s8[4194304]{0:T(1024)(128)(4,1)S(1)}, s32[]{:S(2)}) async-start(s8[8388608]{0:T(1024)(128)(4,1)} %bitcast.26), calls=%async_computation.10 | async-start | bytes 8388608
  138.0 4.3 %slice-start.1 = ((s8[8388608]{0:T(1024)(128)(4,1)}), s8[4194304]{0:T(1024)(128)(4,1)S(1)}, s32[]{:S(2)}) async-start(s8[8388608]{0:T(1024)(128)(4,1)} %bitcast.26), calls=%async_computation.11 | async-start | bytes 8388608
  216.1 76.0 %reduce-scatter.6.cloned.1.call-start = ((), (), s32[]{:S(2)}) async-start(), calls=%async_computation.5 | async-start | bytes 6291456 | tf_op jit(solution)/shard_map/reduce_scatter | solution.py:216
  234.2 103.9 %reduce-scatter.8.cloned.1.call-start = ((), (), s32[]{:S(2)}) async-start(), calls=%async_computation.6 | async-start | bytes 2621440 | tf_op jit(solution)/shard_map/reduce_scatter | solution.py:217
  292.1 70.2 %all-gather.9.cloned.1.call-start = ((), (), s32[]{:S(2)}) async-start(), calls=%async_computation.7 | async-start | bytes 2621440 | tf_op jit(solution)/shard_map/all_gather | solution.py:219
Sparse Core Ops, SparseCore 0:
  8.9 48.6 all-gather.6
  59.2 55.4 all-gather.10
  116.2 19.8 all-gather.12
  216.2 17.9 reduce-scatter.3
  236.5 55.5 reduce-scatter.5
  294.2 43.8 reduce-scatter.7
  340.3 21.8 all-gather.8

commit v2 on v1

--- a/solution.py
+++ b/solution.py
@@ -195,29 +195,410 @@
     )(home, block, index, coeff.reshape(TPD, 2 * K), weight, sky, obs, *bank)
 
 
+MESH = pl.DeviceIdType.MESH
+CHUNKS = 2
+
+
+def greet(strips, visits, bands):
+    me, v, b = (lax.axis_index(a) for a in ("strip", "visit", "band"))
+    barrier = pltpu.get_barrier_semaphore()
+
+    def signal(axis, other):
+        pl.semaphore_signal(barrier, inc=1, device_id={axis: other}, device_id_type=MESH)
+
+    @pl.when(me > 0)
+    def _():
+        signal("strip", me - 1)
+
+    @pl.when(me < strips - 1)
+    def _():
+        signal("strip", me + 1)
+
+    for e in range(1, visits):
+        signal("visit", lax.rem(v + e, visits))
+    for e in range(1, bands):
+        signal("band", lax.rem(b + e, bands))
+
+    peers = visits + bands - 2 + (me > 0).astype(jnp.int32) + (me < strips - 1).astype(jnp.int32)
+    pl.semaphore_wait(barrier, peers)
+
+
+def gather_kernel(
+    strips, visits, bands, sky, out, edge, side,
+    own_sem, edge_sem, side_sem, zs, zr, xs, xr, bs, br,
+):
+    me, v, b = (lax.axis_index(a) for a in ("strip", "visit", "band"))
+    piece = PW // (visits * bands)
+    height = SROWS // CHUNKS
+    other = lax.rem(b + 1, bands)
+    edge[...] = jnp.zeros_like(edge)
+    side[...] = jnp.zeros_like(side)
+    local = [
+        pltpu.make_async_copy(
+            sky,
+            out.at[pl.ds(pl.multiple_of(R + me * SROWS, 8), SROWS), pl.ds(LANE, PW)],
+            own_sem,
+        ),
+        pltpu.make_async_copy(edge, out.at[pl.ds(0, R)], edge_sem.at[0]),
+        pltpu.make_async_copy(edge, out.at[pl.ds(R + strips * SROWS, R)], edge_sem.at[1]),
+    ]
+    for s in range(strips):
+        rows = pl.ds(R + s * SROWS, SROWS)
+        local.append(pltpu.make_async_copy(side, out.at[rows, pl.ds(0, LANE)], side_sem.at[0, s]))
+        local.append(
+            pltpu.make_async_copy(side, out.at[rows, pl.ds(LANE + PW, LANE)], side_sem.at[1, s])
+        )
+    greet(strips, visits, bands)
+
+    def spot(s, c, h):
+        return out.at[
+            pl.ds(pl.multiple_of(R + s * SROWS + h * height, 8), height),
+            pl.ds(pl.multiple_of(LANE + c * piece, LANE), piece),
+        ]
+
+    def remote(src, dst, send, recv, axis, target):
+        return pltpu.make_async_remote_copy(
+            src_ref=src, dst_ref=dst, send_sem=send, recv_sem=recv,
+            device_id={axis: target}, device_id_type=MESH,
+        )
+
+    mine = v * bands + b
+
+    def hop(way, d, h, incoming):
+        sign = 1 if way == 0 else -1
+        s = me - sign * (d if incoming else d - 1)
+        dst = spot(s, mine, h)
+        if d == 1 and not incoming:
+            src = sky.at[
+                pl.ds(h * height, height), pl.ds(pl.multiple_of(mine * piece, LANE), piece)
+            ]
+        else:
+            src = dst
+        return remote(src, dst, zs.at[way, d - 1, h], zr.at[way, d - 1, h], "strip", me + sign)
+
+    def can_send(way, d):
+        return (me < strips - 1) & (me >= d - 1) if way == 0 else (me > 0) & (me + d - 1 < strips)
+
+    def can_get(way, d):
+        return me >= d if way == 0 else me + d < strips
+
+    def across(way, d, h, e, incoming):
+        s = me - d if way == 0 else me + d
+        owner = lax.rem(v - e + visits, visits) if incoming else v
+        at = spot(s, owner * bands + b, h)
+        return remote(
+            at, at, xs.at[way, d - 1, h, e - 1], xr.at[way, d - 1, h, e - 1],
+            "visit", lax.rem(v + e, visits),
+        )
+
+    def beside(way, d, h, e, incoming):
+        s = me - d if way == 0 else me + d
+        at = spot(s, lax.rem(v - e + visits, visits) * bands + (other if incoming else b), h)
+        return remote(at, at, bs.at[way, d - 1, h, e], br.at[way, d - 1, h, e], "band", other)
+
+    for h in range(CHUNKS):
+        for way in range(2):
+
+            @pl.when(can_send(way, 1))
+            def _():
+                hop(way, 1, h, False).start()
+
+    for copy in local:
+        copy.start()
+    for d in range(1, strips):
+        for h in range(CHUNKS):
+            for way in range(2):
+
+                @pl.when(can_get(way, d))
+                def _():
+                    hop(way, d, h, True).wait_recv()
+                    if d + 1 < strips:
+
+                        @pl.when(can_send(way, d + 1))
+                        def _():
+                            hop(way, d + 1, h, False).start()
+
+                    for e in range(1, visits):
+                        across(way, d, h, e, False).start()
+                    beside(way, d, h, 0, False).start()
+
+        for h in range(CHUNKS):
+            for way in range(2):
+                if d < 2:
+                    continue
+
+                @pl.when(can_get(way, d - 1))
+                def _():
+                    for e in range(1, visits):
+                        across(way, d - 1, h, e, True).wait_recv()
+                        beside(way, d - 1, h, e, False).start()
+
+    for h in range(CHUNKS):
+        for way in range(2):
+
+            @pl.when(can_get(way, strips - 1))
+            def _():
+                for e in range(1, visits):
+                    across(way, strips - 1, h, e, True).wait_recv()
+                    beside(way, strips - 1, h, e, False).start()
+
+    for d in range(1, strips):
+        for h in range(CHUNKS):
+            for way in range(2):
+
+                @pl.when(can_send(way, d))
+                def _():
+                    hop(way, d, h, False).wait_send()
+
+                @pl.when(can_get(way, d))
+                def _():
+                    for e in range(1, visits):
+                        across(way, d, h, e, False).wait_send()
+                    for e in range(visits):
+                        beside(way, d, h, e, False).wait_send()
+                        beside(way, d, h, e, True).wait_recv()
+
+    for copy in local:
+        copy.wait()
+
+
+def gather_sky(sky, strips, visits, bands):
+    dma = pltpu.SemaphoreType.DMA
+    hbm = pl.BlockSpec(memory_space=pl.ANY)
+    steps = strips - 1
+    return pl.pallas_call(
+        functools.partial(gather_kernel, strips, visits, bands),
+        out_shape=jax.ShapeDtypeStruct((strips * SROWS + 2 * R, MW), f32),
+        in_specs=[hbm],
+        out_specs=hbm,
+        scratch_shapes=[
+            pltpu.VMEM((R, MW), f32),
+            pltpu.VMEM((SROWS, LANE), f32),
+            dma,
+            dma((2,)),
+            dma((2, strips)),
+            dma((2, steps, CHUNKS)),
+            dma((2, steps, CHUNKS)),
+            dma((2, steps, CHUNKS, visits - 1)),
+            dma((2, steps, CHUNKS, visits - 1)),
+            dma((2, steps, CHUNKS, visits)),
+            dma((2, steps, CHUNKS, visits)),
+        ],
+        compiler_params=pltpu.CompilerParams(collective_id=0, has_side_effects=True),
+    )(sky)
+
+
+def reduce_kernel(
+    strips, visits, bands, grad, sky, out, loc, bbuf, xbuf, zbuf, mine, new,
+    loc_sem, mine_sem, new_sem, bs, br, xs, xr, zs, zr, ns, nr, ps, pr,
+):
+    me, v, b = (lax.axis_index(a) for a in ("strip", "visit", "band"))
+    piece = PW // (visits * bands)
+    other = lax.rem(b + 1, bands)
+
+    def columns(c, margin):
+        return pl.ds(pl.multiple_of(margin + c * piece, LANE), piece)
+
+    def spot(s, c):
+        return grad.at[pl.ds(pl.multiple_of(R + s * SROWS, 8), SROWS), columns(c, LANE)]
+
+    def remote(src, dst, send, recv, axis, target):
+        return pltpu.make_async_remote_copy(
+            src_ref=src, dst_ref=dst, send_sem=send, recv_sem=recv,
+            device_id={axis: target}, device_id_type=MESH,
+        )
+
+    order = [(way, d) for d in range(strips - 1, 0, -1) for way in range(2)] + [(0, 0)]
+
+    def strip_of(way, d):
+        return me + d if way == 0 else me - d
+
+    def there(way, d):
+        return me + d < strips if way == 0 else me >= d
+
+    def visit_at(e):
+        return lax.rem(v + e, visits)
+
+    def load(j, s, e):
+        return pltpu.make_async_copy(
+            spot(s, visit_at(e) * bands + b), loc.at[s, e], loc_sem.at[j, e]
+        )
+
+    def beside(j, s, e):
+        return remote(
+            spot(s, visit_at(e) * bands + other), bbuf.at[s, e],
+            bs.at[j, e], br.at[j, e], "band", other,
+        )
+
+    def across(j, s, e):
+        return remote(
+            loc.at[s, e], xbuf.at[s, e - 1], xs.at[j, e - 1], xr.at[j, e - 1],
+            "visit", visit_at(e),
+        )
+
+    def hop(way, d):
+        sign = 1 if way == 0 else -1
+        s = strip_of(way, d)
+        return remote(
+            loc.at[s, 0], zbuf.at[way, s], zs.at[way, d - 1], zr.at[way, d - 1],
+            "strip", me + sign,
+        )
+
+    def came(way, d):
+        sign = 1 if way == 0 else -1
+        s = strip_of(way, d)
+        return remote(
+            loc.at[s, 0], zbuf.at[way, s], zs.at[way, d], zr.at[way, d], "strip", me - sign
+        )
+
+    def behind(way):
+        return me > 0 if way == 0 else me < strips - 1
+
+    keep = pltpu.make_async_copy(sky.at[:, columns(v * bands + b, 0)], mine, mine_sem)
+    greet(strips, visits, bands)
+    for j, (way, d) in enumerate(order):
+
+        @pl.when(there(way, d))
+        def _():
+            s = strip_of(way, d)
+            for e in [*range(1, visits), 0]:
+                beside(j, s, e).start()
+                load(j, s, e).start()
+
+    keep.start()
+
+    def first(j, way, d):
+        s = strip_of(way, d)
+        for e in [*range(1, visits), 0]:
+            load(j, s, e).wait()
+            beside(j, s, e).wait_recv()
+            loc[s, e] = loc[s, e] + bbuf[s, e]
+            if e:
+                across(j, s, e).start()
+
+    def second(j, way, d):
+        s = strip_of(way, d)
+        for e in range(1, visits):
+            across(j, s, e).wait_recv()
+            loc[s, 0] = loc[s, 0] + xbuf[s, e - 1]
+        if d:
+
+            @pl.when(behind(way))
+            def _():
+                came(way, d).wait_recv()
+                loc[s, 0] = loc[s, 0] + zbuf[way, s]
+
+            hop(way, d).start()
+
+    for j, (way, d) in enumerate(order):
+
+        @pl.when(there(way, d))
+        def _():
+            first(j, way, d)
+
+    for j, (way, d) in enumerate(order):
+
+        @pl.when(there(way, d))
+        def _():
+            second(j, way, d)
+
+    for way in range(2):
+
+        @pl.when(behind(way))
+        def _():
+            came(way, 0).wait_recv()
+            loc[me, 0] = loc[me, 0] + zbuf[way, me]
+
+    keep.wait()
+    new[...] = jnp.maximum(mine[...] - step_size * loc[me, 0], 0.0)
+
+    def place(c):
+        return out.at[:, columns(c, 0)]
+
+    own = v * bands + b
+    write = pltpu.make_async_copy(new, place(own), new_sem)
+
+    def spread(e, incoming):
+        c = lax.rem(v - e + visits, visits) * bands + b if incoming else own
+        return remote(new, place(c), ns.at[e - 1], nr.at[e - 1], "visit", visit_at(e))
+
+    def passed(e, incoming):
+        c = lax.rem(v - e + visits, visits) * bands
+        dst = place(c + (other if incoming else b))
+        return remote(new if e == 0 else dst, dst, ps.at[e], pr.at[e], "band", other)
+
+    for e in range(1, visits):
+        spread(e, False).start()
+    passed(0, False).start()
+    write.start()
+    for e in range(1, visits):
+        spread(e, True).wait_recv()
+        passed(e, False).start()
+    for e in range(visits):
+        passed(e, True).wait_recv()
+        passed(e, False).wait_send()
+    for e in range(1, visits):
+        spread(e, False).wait_send()
+    write.wait()
+    for j, (way, d) in enumerate(order):
+
+        @pl.when(there(way, d))
+        def _():
+            s = strip_of(way, d)
+            for e in range(visits):
+                beside(j, s, e).wait_send()
+                if e:
+                    across(j, s, e).wait_send()
+            if d:
+                hop(way, d).wait_send()
+
+
+def reduce_gradient(grad, sky, strips, visits, bands):
+    dma = pltpu.SemaphoreType.DMA
+    hbm = pl.BlockSpec(memory_space=pl.ANY)
+    piece = PW // (visits * bands)
+    number = 2 * strips - 1
+    block = (SROWS, piece)
+    return pl.pallas_call(
+        functools.partial(reduce_kernel, strips, visits, bands),
+        out_shape=jax.ShapeDtypeStruct(sky.shape, f32),
+        in_specs=[hbm, hbm],
+        out_specs=hbm,
+        scratch_shapes=[
+            pltpu.VMEM((strips, visits) + block, f32),
+            pltpu.VMEM((strips, visits) + block, f32),
+            pltpu.VMEM((strips, visits - 1) + block, f32),
+            pltpu.VMEM((2, strips) + block, f32),
+            pltpu.VMEM(block, f32),
+            pltpu.VMEM(block, f32),
+            dma((number, visits)),
+            dma,
+            dma,
+            dma((number, visits)),
+            dma((number, visits)),
+            dma((number, visits - 1)),
+            dma((number, visits - 1)),
+            dma((2, strips)),
+            dma((2, strips)),
+            dma((visits - 1,)),
+            dma((visits - 1,)),
+            dma((visits,)),
+            dma((visits,)),
+        ],
+        compiler_params=pltpu.CompilerParams(
+            collective_id=1, has_side_effects=True, vmem_limit_bytes=60 * 2**20
+        ),
+    )(grad, sky)
+
+
 def on_device(observed, home_strip, column_block, psf_index, psf_coeff, weight, kernels, sky_model):
-    visits, bands = lax.axis_size("visit"), lax.axis_size("band")
-    piece = PW // (visits * bands)
-    at = (lax.axis_index("visit") * bands + lax.axis_index("band")) * piece
-    mine = lax.dynamic_slice_in_dim(sky_model, at, piece, 1)
-    whole = lax.all_gather(mine, "strip", axis=0, tiled=True)
-    whole = lax.all_gather(whole, "visit", axis=0)
-    whole = lax.all_gather(whole, "band", axis=1)
-    sky = jnp.zeros((whole.shape[2] + 2 * R, MW), f32)
-    for v in range(visits):
-        for b in range(bands):
-            sky = lax.dynamic_update_slice(sky, whole[v, b], (R, LANE + (v * bands + b) * piece))
+    sizes = [lax.axis_size(a) for a in ("strip", "visit", "band")]
     bank = banks(kernels)
+    sky = gather_sky(sky_model, *sizes)
     grads = tile_gradients(
         home_strip, column_block, psf_index, psf_coeff, weight, sky, observed, bank
     )
-    grads = grads[R:-R, LANE:-LANE].reshape(-1, visits, bands, piece).transpose(2, 1, 0, 3)
-    grads = lax.psum_scatter(grads, "band", scatter_dimension=0)
-    grads = lax.psum_scatter(grads, "visit", scatter_dimension=0)
-    grads = lax.psum_scatter(grads, "strip", scatter_dimension=0, tiled=True)
-    new = jnp.maximum(mine - step_size * grads, 0.0)
-    new = lax.all_gather(new, ("visit", "band"), axis=1, tiled=True)
-    return new
+    return reduce_gradient(grads, sky_model, *sizes)
 
 
 def solution(mesh):

time: 373 us -> 196 us (0.53)
  waiting for transfers between devices: 259 us -> 0 us
  Pallas kernels: 38.4 us -> 176 us
  local copies, waits for them, and re-layouts: 49.4 us -> 8.79 us
  between operations: 13.7 us -> 0.18 us
    pallas_call x0 -> x2, Pallas kernels: none -> 137 us  [the longest x1 68.7 us: reduce_gradient(): pl.pallas_call(functools.partial(reduce_kernel, strips, visits, bands), o...]
    all_gather x4 -> x0, waiting for transfers between devices: 137 us -> none  [the longest x1 57 us: on_device(): whole = lax.all_gather(whole, 'visit', axis=0)]
    reduce_scatter x3 -> x0, waiting for transfers between devices: 122 us -> none  [the longest x1 57.8 us: on_device(): grads = lax.psum_scatter(grads, 'visit', scatter_dimension=0)]
    reshape x2 -> x0, local copies, waits for them, and re-layouts: 23.2 us -> none  [on_device(): grads[R:-R, LANE:-LANE].reshape(-1, visits, bands, piece)]
    dynamic_update_slice x4 -> x0, local copies, waits for them, and re-layouts: 8.82 us -> none  [on_device(): lax.dynamic_update_slice(sky, whole[v, b], (R, LANE + (v * bands + b) * p...]
    slice x1 -> x0, local copies, waits for them, and re-layouts: 7.63 us -> none  [on_device(): grads[R:-R, LANE:-LANE].reshape(-1, visits, bands, piece)]
  transfers between devices with their start and end apart: 7 -> 0, of which waited for: 7 -> 0; matrix products, arithmetic and copies ran while one was open for 3% -> 0% of each run, Pallas kernels for 0% -> 0%
where the time goes in v2:
time: 196 us; the launch traced here: 194 us
  Pallas kernels  176 us (90%)
  other arithmetic  9.27 us (5%)
  local copies, waits for them, and re-layouts  8.79 us (4%)
    pallas_call x1, Pallas kernels, reduce_gradient(): pl.pallas_call(functools.partial(reduce_kernel, strips, visits, bands), o...  68.7 us
    pallas_call x1, Pallas kernels, gather_sky(): pl.pallas_call(functools.partial(gather_kernel, strips, visits, bands), o...  68.6 us
    pallas_call x1, Pallas kernels, tile_gradients(): pl.pallas_call(tiles_kernel, out_shape=jax.ShapeDtypeStruct(sky.shape, f3...  38.4 us
    unnamed x3, local copies, waits for them, and re-layouts  5.79 us
    convert_element_type x4, other arithmetic, split_outside(): return (hi.astype(bf16), (x - hi).astype(bf16))  4.76 us

profile of v2, /device:TPU:0, one launch (start us, length us, event | category | flops | bytes accessed | tf_op | source)
XLA Modules:
  0.0 194.1 jit_solution(14097197850500506303)
XLA Ops:
  0.0 1.3 copy.12.home
  1.3 1.3 copy.13.index
  2.7 1.4 copy.14.coeff
  4.0 0.8 fusion.41
  4.8 0.4 slice_reduce_fusion.33
  5.3 0.4 slice_reduce_fusion.16
  6.3 2.4 %select_add_fusion.1.colt = f32[8,144,128]{2,1,0:T(8,128)} fusion(f32[8]{0:T(128)S(1)} %get-tuple-element.6, f32[8]{0:T(128)S(1)} %get-tuple-element.7, f32[8]{0:T(128)S(1)} %get-tuple-element.8, f32[8]{0:T(128)S(1)} %get-tuple-element.9, f32[8]{0:T(128)S(1)} %get-tuple-element.10, f32[8]{0:T(128)S(1)} %get-tuple-element.11, f32[8]{0:T(128)S(1)} %get-tuple-element.12, ...), kind=kLoop, calls=%fused_computation.13 | loop fusion | flops 4866048 | bytes 903712 | tf_op jit(solution)/shard_map/add | solution.py:42
  8.7 2.2 %fusion.6 = (bf16[8,144,128]{2,1,0:T(8,128)(2,1)}, f32[8,144,128]{2,1,0:T(8,128)S(1)}) fusion(f32[8]{0:T(128)S(1)} %get-tuple-element.23, pred[144,128]{1,0:T(8,128)(4,1)S(1)} %get-tuple-element.61, f32[8]{0:T(128)S(1)} %get-tuple-element.24, pred[144,128]{1,0:T(8,128)(4,1)S(1)} %get-tuple-element.62, f32[8]{0:T(128)S(1)} %get-tuple-element.25, ...), kind=kLoop, calls=%fused_computation.12 | loop fusion | flops 5308416 | bytes 1198624 | tf_op jit(solution)/shard_map/convert_element_type | solution.py:33
  11.0 0.7 reduce-precision_convert_fusion.1.thi
  11.7 1.7 fusion.3
  13.4 0.1 reduce-precision_convert_fusion
  13.5 1.6 fusion.5.prow
  15.1 68.6 %shard_map.82.sky = f32[528,4352]{1,0:T(8,128)} custom-call(f32[128,4096]{1,0:T(8,128)} %sky.3), custom_call_target="tpu_custom_call" | custom-call | tf_op jit(solution)/shard_map/pallas_call | solution.py:369
  83.8 38.4 %shard_map.83.grad = f32[528,4352]{1,0:T(8,128)} custom-call(s32[16,1]{1,0:T(8,128)} %copy.12.home, s32[16]{0:T(128)} %block.1, s32[16,4]{1,0:T(8,128)} %copy.13.index, f32[16,8]{1,0:T(8,128)} %copy.14.coeff, f32[16]{0:T(128)} %weight.1, f32[528,4352]{1,0:T(8,128)} %shard_map.82.sky, f32[16,128,512]{2,1,0:T(8,128)} %obs.1, bf16[8,128,512]{2,1,0:T(8,128)(2,1)} %fusion.5.prow, ...), custom_call_target="tpu_custom_call" | custom-call | tf_op jit(solution)/shard_map/pallas_call | solution.py:174
  122.2 68.7 %shard_map.84 = f32[128,4096]{1,0:T(8,128)} custom-call(f32[528,4352]{1,0:T(8,128)} %shard_map.83.grad, f32[128,4096]{1,0:T(8,128)} %sky.3), custom_call_target="tpu_custom_call" | custom-call | tf_op jit(solution)/shard_map/pallas_call | solution.py:562
  191.0 3.1 %copy.16 = f32[128,4096]{1,0:T(8,128)} copy(f32[128,4096]{1,0:T(8,128)} %shard_map.84) | data formatting | bytes 4194304
  (18 shorter events, 0.5 us)

commit v3 on v2

--- a/solution.py
+++ b/solution.py
@@ -28,30 +28,27 @@
     return hi, (x - hi.astype(f32)).astype(bf16)
 
 
-def split_outside(x):
-    hi = lax.reduce_precision(x, 8, 7)
-    return hi.astype(bf16), (x - hi).astype(bf16)
-
-
-def banded(taps, height, breadth, offset_of):
-    rows = lax.broadcasted_iota(jnp.int32, (1, height, breadth), 1)
-    cols = lax.broadcasted_iota(jnp.int32, (1, height, breadth), 2)
-    distance = offset_of(rows, cols)
-    total = jnp.zeros((taps.shape[0], height, breadth), f32)
-    for d in range(taps.shape[1]):
-        total = total + jnp.where(distance == d, taps[:, d][:, None, None], 0.0)
+def tap_sum(taps, n, side, distance):
+    total = jnp.zeros(distance.shape, f32)
+    for d in range(2 * R + 1):
+        total = total + jnp.where(distance == d, taps[n, side * (2 * R + 1) + d], 0.0)
     return total
 
 
-def banks(kernels):
-    row = banded(kernels[:, 0], SROWS, REACH, lambda i, j: j - i)
-    rowt = banded(kernels[:, 0], REACH, SROWS, lambda j, i: j - i)
-    colt = banded(kernels[:, 1], REACH, LANE, lambda c, b: c - b)
-    hi, lo = split_outside(row)
-    prow = jnp.concatenate([hi, lo, hi], 2)
-    prow = jnp.pad(prow, ((0, 0), (0, 0), (0, 512 - 3 * REACH)))
-    thi, tlo = split_outside(rowt)
-    return prow, thi, tlo, colt
+def build_bank(n, taps, prow, thi, tlo, colt):
+    i = lax.broadcasted_iota(jnp.int32, (SROWS, 512), 0)
+    j = lax.broadcasted_iota(jnp.int32, (SROWS, 512), 1)
+    second, third = j >= REACH, j >= 2 * REACH
+    at = j - jnp.where(second, REACH, 0) - jnp.where(third, REACH, 0)
+    total = tap_sum(taps, n, 0, jnp.where(j < 3 * REACH, at - i, -1))
+    hi = total.astype(bf16).astype(f32)
+    prow[n] = jnp.where(second & ~third, total - hi, hi).astype(bf16)
+    rows = lax.broadcasted_iota(jnp.int32, (REACH, LANE), 0)
+    distance = rows - lax.broadcasted_iota(jnp.int32, (REACH, LANE), 1)
+    hi, lo = split(tap_sum(taps, n, 0, distance))
+    thi[n] = hi
+    tlo[n] = lo
+    colt[n] = tap_sum(taps, n, 1, distance)
 
 
 def mm(a, b):
@@ -63,7 +60,7 @@
 
 
 def tiles_kernel(
-    home, block, index, coeff, weight, sky, obs, prow, thi, tlo, colt,
+    meta, sky, obs, prow, thi, tlo, colt,
     acc, wcat, pcat, lhi, llo, qhi, qlo, bhi, blo, pthi, ptlo, views, seen, sems,
 ):
     acc[...] = jnp.zeros_like(acc)
@@ -78,8 +75,8 @@
 
     def fetches(i):
         t, slot = band * count + i, i % 2
-        top = pl.multiple_of(home[t, 0] * SROWS, SROWS)
-        start = pl.multiple_of(block[t] * LANE, LANE)
+        top = pl.multiple_of(meta[t].astype(jnp.int32) * SROWS, SROWS)
+        start = pl.multiple_of(meta[TPD + t].astype(jnp.int32) * LANE, LANE)
         return (
             pltpu.make_async_copy(
                 sky.at[pl.ds(top, REACH), pl.ds(start, VIEW)], views.at[slot], sems.at[0, slot]
@@ -100,21 +97,21 @@
 
         for copy in fetches(i):
             copy.wait()
-        top = pl.multiple_of(home[t, 0] * SROWS, SROWS)
-        start = pl.multiple_of(block[t] * LANE, LANE)
+        top = pl.multiple_of(meta[t].astype(jnp.int32) * SROWS, SROWS)
+        start = pl.multiple_of(meta[TPD + t].astype(jnp.int32) * LANE, LANE)
         window = pltpu.roll(views[slot], VIEW - (LANE - R), 1)[:, :EXT]
         whi, wlo = split(window)
         wcat[0:REACH, :] = whi
         wcat[REACH : 2 * REACH, :] = whi
         wcat[2 * REACH : 3 * REACH, :] = wlo
         for k in range(K):
-            n = index[t, k]
+            n = meta[2 * TPD + t * K + k].astype(jnp.int32)
             pcat[k * SROWS : (k + 1) * SROWS, :] = prow[n]
             pthi[:, k * SROWS : (k + 1) * SROWS] = thi[n]
             ptlo[:, k * SROWS : (k + 1) * SROWS] = tlo[n]
             taps = colt[n]
             for half in range(2):
-                hi, lo = split(taps * coeff[t, 2 * k + half])
+                hi, lo = split(taps * meta[(2 + K) * TPD + t * 2 * K + 2 * k + half])
                 side = slice(half * LANE, (half + 1) * LANE)
                 qhi[k * LANE : (k + 1) * LANE, side] = hi[:LANE]
                 qlo[k * LANE : (k + 1) * LANE, side] = lo[:LANE]
@@ -136,7 +133,7 @@
             lhi[rows, K * LANE :] = hi
             llo[rows, K * LANE :] = lo
         both = mm(lhi[...], qhi[...]) + mm(lhi[...], qlo[...]) + mm(llo[...], qhi[...])
-        factor = weight[t]
+        factor = meta[(2 + 3 * K) * TPD + t]
         spread = []
         for q in range(TW // LANE):
             rows = slice(q * LANE, (q + 1) * LANE)
@@ -171,10 +168,12 @@
 def tile_gradients(home, block, index, coeff, weight, sky, obs, bank):
     vmem = pl.BlockSpec(memory_space=pltpu.VMEM)
     smem = pl.BlockSpec(memory_space=pltpu.SMEM)
+    parts = (home.astype(f32), block.astype(f32), index.astype(f32), coeff, weight)
+    meta = jnp.concatenate([x.reshape(-1) for x in parts])
     return pl.pallas_call(
         tiles_kernel,
         out_shape=jax.ShapeDtypeStruct(sky.shape, f32),
-        in_specs=[smem] * 5 + [pl.BlockSpec(memory_space=pl.ANY)] * 2 + [vmem] * 4,
+        in_specs=[smem] + [pl.BlockSpec(memory_space=pl.ANY)] * 2 + [vmem] * 4,
         out_specs=vmem,
         scratch_shapes=[
             pltpu.VMEM((512, EXT), bf16),
@@ -192,11 +191,11 @@
             pltpu.SemaphoreType.DMA((2, 2)),
         ],
         compiler_params=pltpu.CompilerParams(vmem_limit_bytes=56 * 2**20),
-    )(home, block, index, coeff.reshape(TPD, 2 * K), weight, sky, obs, *bank)
+    )(meta, sky, obs, *bank)
 
 
 MESH = pl.DeviceIdType.MESH
-CHUNKS = 2
+CHUNKS = 4
 
 
 def greet(strips, visits, bands):
@@ -224,7 +223,7 @@
 
 
 def gather_kernel(
-    strips, visits, bands, sky, out, edge, side,
+    strips, visits, bands, sky, taps, out, prow, thi, tlo, colt, edge, side,
     own_sem, edge_sem, side_sem, zs, zr, xs, xr, bs, br,
 ):
     me, v, b = (lax.axis_index(a) for a in ("strip", "visit", "band"))
@@ -322,6 +321,14 @@
                         across(way, d, h, e, False).start()
                     beside(way, d, h, 0, False).start()
 
+        if d == 1:
+
+            def build(n, carry):
+                build_bank(n, taps, prow, thi, tlo, colt)
+                return carry
+
+            lax.fori_loop(0, prow.shape[0], build, 0)
+
         for h in range(CHUNKS):
             for way in range(2):
                 if d < 2:
@@ -362,15 +369,22 @@
         copy.wait()
 
 
-def gather_sky(sky, strips, visits, bands):
+def gather_sky(sky, kernels, strips, visits, bands):
     dma = pltpu.SemaphoreType.DMA
     hbm = pl.BlockSpec(memory_space=pl.ANY)
-    steps = strips - 1
+    vmem = pl.BlockSpec(memory_space=pltpu.VMEM)
+    steps, count = strips - 1, kernels.shape[0]
     return pl.pallas_call(
         functools.partial(gather_kernel, strips, visits, bands),
-        out_shape=jax.ShapeDtypeStruct((strips * SROWS + 2 * R, MW), f32),
-        in_specs=[hbm],
-        out_specs=hbm,
+        out_shape=(
+            jax.ShapeDtypeStruct((strips * SROWS + 2 * R, MW), f32),
+            jax.ShapeDtypeStruct((count, SROWS, 512), bf16),
+            jax.ShapeDtypeStruct((count, REACH, LANE), bf16),
+            jax.ShapeDtypeStruct((count, REACH, LANE), bf16),
+            jax.ShapeDtypeStruct((count, REACH, LANE), f32),
+        ),
+        in_specs=[hbm, pl.BlockSpec(memory_space=pltpu.SMEM)],
+        out_specs=(hbm, vmem, vmem, vmem, vmem),
         scratch_shapes=[
             pltpu.VMEM((R, MW), f32),
             pltpu.VMEM((SROWS, LANE), f32),
@@ -384,8 +398,8 @@
             dma((2, steps, CHUNKS, visits)),
             dma((2, steps, CHUNKS, visits)),
         ],
-        compiler_params=pltpu.CompilerParams(collective_id=0, has_side_effects=True),
-    )(sky)
+        compiler_params=pltpu.CompilerParams(collective_id=0, has_side_effects=True, vmem_limit_bytes=24 * 2**20),
+    )(sky, kernels.reshape(count, -1))
 
 
 def reduce_kernel(
@@ -593,8 +607,7 @@
 
 def on_device(observed, home_strip, column_block, psf_index, psf_coeff, weight, kernels, sky_model):
     sizes = [lax.axis_size(a) for a in ("strip", "visit", "band")]
-    bank = banks(kernels)
-    sky = gather_sky(sky_model, *sizes)
+    sky, *bank = gather_sky(sky_model, kernels, *sizes)
     grads = tile_gradients(
         home_strip, column_block, psf_index, psf_coeff, weight, sky, observed, bank
     )

time: 196 us -> 172 us (0.88)
  Pallas kernels: 176 us -> 154 us
  other arithmetic: 9.27 us -> 2 us
  local copies, waits for them, and re-layouts: 8.79 us -> 14.7 us
    pallas_call x1, Pallas kernels: 68.6 us -> 49.1 us  [gather_sky(): pl.pallas_call(functools.partial(gather_kernel, strips, visits, bands), o...]
    unnamed x3 -> x14, local copies, waits for them, and re-layouts: 5.79 us -> 12.3 us
    convert_element_type x4 -> x2, other arithmetic: 4.76 us -> 1.34 us  [the longest x1 0.68 us: tile_gradients(): index.astype(f32)]
    add x1 -> x0, other arithmetic: 2.4 us -> none  [banded(): total = total + jnp.where(distance == d, taps[:, d][:, None, None], 0.0)]
where the time goes in v3:
time: 172 us; the launch traced here: 171 us
  Pallas kernels  154 us (90%)
  local copies, waits for them, and re-layouts  14.7 us (9%)
  other arithmetic  2 us (1%)
    pallas_call x1, Pallas kernels, reduce_gradient(): pl.pallas_call(functools.partial(reduce_kernel, strips, visits, bands), o...  66.9 us
    pallas_call x1, Pallas kernels, gather_sky(): pl.pallas_call(functools.partial(gather_kernel, strips, visits, bands), o...  49.1 us
    pallas_call x1, Pallas kernels, tile_gradients(): pl.pallas_call(tiles_kernel, out_shape=jax.ShapeDtypeStruct(sky.shape, f3...  38.5 us
    unnamed x14, local copies, waits for them, and re-layouts  12.3 us

profile of v3, /device:TPU:0, one launch (start us, length us, event | category | flops | bytes accessed | tf_op | source)
XLA Modules:
  0.0 171.1 jit_solution(2944067690351769065)
XLA Ops:
  0.0 0.7 convert_bitcast_fusion
  0.7 0.7 convert_element_type.10
  1.3 0.7 convert_element_type.11
  2.0 0.8 reshape.15.taps
  2.8 0.1 copy.11
  2.9 0.1 reshape.13
  2.9 0.8 copy.12
  3.7 0.1 reshape.14
  3.9 1.3 concatenate.3.meta
  5.2 0.0 copy-start.1
  5.2 1.6 copy-done.1
  6.8 49.1 %shard_map.82 = (f32[528,4352]{1,0:T(8,128)S(1)}, bf16[8,128,512]{2,1,0:T(8,128)(2,1)S(1)}, bf16[8,144,128]{2,1,0:T(8,128)(2,1)S(1)}, bf16[8,144,128]{2,1,0:T(8,128)(2,1)S(1)}, f32[8,144,128]{2,1,0:T(8,128)S(1)}) custom-call(f32[128,4096]{1,0:T(8,128)S(1)} %copy-done.1, f32[8,34]{1,0:T(8,128)S(1)} %reshape.15.taps), custom_call_target="tpu_custom_call" | custom-call | tf_op jit(solution)/shard_map/pallas_call | solution.py:377
  55.9 0.0 copy-start
  55.9 3.5 %copy-done = f32[528,4352]{1,0:T(8,128)} copy-done((f32[528,4352]{1,0:T(8,128)}, f32[528,4352]{1,0:T(8,128)S(1)}, u32[]{:S(2)}) %copy-start) | copy-done | bytes 9191448
  59.4 0.0 copy-start.2
  59.4 1.0 copy-done.2
  60.4 0.0 copy-start.3
  60.4 0.8 copy-done.3
  61.2 0.0 copy-start.4
  61.2 0.7 copy-done.4
  61.9 0.0 copy-start.5
  61.9 0.7 copy-done.5
  62.7 38.5 %shard_map.83.grad = f32[528,4352]{1,0:T(8,128)} custom-call(f32[240]{0:T(256)} %concatenate.3.meta, f32[528,4352]{1,0:T(8,128)} %copy-done, f32[16,128,512]{2,1,0:T(8,128)} %obs.1, bf16[8,128,512]{2,1,0:T(8,128)(2,1)} %copy-done.2, bf16[8,144,128]{2,1,0:T(8,128)(2,1)} %copy-done.4, bf16[8,144,128]{2,1,0:T(8,128)(2,1)} %copy-done.5, f32[8,144,128]{2,1,0:T(8,128)} %copy-done.3), custom_call_target="tpu_custom_call" | custom-call | tf_op jit(solution)/shard_map/pallas_call | solution.py:173
  101.1 66.9 %shard_map.84 = f32[128,4096]{1,0:T(8,128)} custom-call(f32[528,4352]{1,0:T(8,128)} %shard_map.83.grad, f32[128,4096]{1,0:T(8,128)} %sky.3), custom_call_target="tpu_custom_call" | custom-call | tf_op jit(solution)/shard_map/pallas_call | solution.py:576
  168.0 3.1 %copy.14 = f32[128,4096]{1,0:T(8,128)} copy(f32[128,4096]{1,0:T(8,128)} %shard_map.84) | data formatting | bytes 4194304
Async XLA Ops:
  5.2 1.6 copy-start.1
  55.9 3.5 %copy-start = (f32[528,4352]{1,0:T(8,128)}, f32[528,4352]{1,0:T(8,128)S(1)}, u32[]{:S(2)}) copy-start(f32[528,4352]{1,0:T(8,128)S(1)} %get-tuple-element.10.sky) | copy-start | bytes 27574276
  59.4 1.0 copy-start.2
  60.4 0.8 copy-start.3
  61.2 0.7 copy-start.4
  61.9 0.7 copy-start.5
